TPU v7x, 32 devices: a whole 2x2x4 slice. The times are simulated.
32 devices in a mesh: copies: 2 (over y), tensor: 8 (over z, x), sub: 2 (over core).
Axes of the slice: x: 2, y: 2, z: 4, core: 2. Of those that a mesh axis runs over, the one named last changes fastest.
Arguments:
- acts: bfloat16 [512, 8192], P(('copies', 'sub'), 'tensor'), parts along dimension 0, may hold values from -6 to 6
- teacher_w: bfloat16 [8192, 8192], P(None, ('tensor', 'sub'))
- student_w: bfloat16 [8192, 8192], P('tensor'), may hold values from -0.09375 to 0.09375
- block_mask: int32 [64, 64], P('tensor'), may hold values from 0 to 1, as said below
Outputs:
- student_grad: float32 [16384, 8192], P(('copies', 'tensor')), parts along dimension 0
- loss: float32 [2], P('copies'), parts along dimension 0
There are 2 independent parts, one for each index of `copies`. A program takes and returns all parts, laid end to end along the dimension named above; an argument that names none is the same for every part. Nothing has to cross between parts.
Inputs may be any that keep to these rules, and one draw needn't show every extreme that they name: `block_mask`: zeros and ones; each block row keeps its own share of blocks.
All inputs are finite; a program needn't handle non-finite values.
Results may differ from a plain program's by a relative error of at most 0.008.
Values may be sent and summed in bfloat16 or wider, within the bound.
A program may use at most 256 MiB of HBM per device.

v0:
```python
import jax
import jax.numpy as jnp
from jax import lax
from jax.sharding import PartitionSpec as P


def shards(acts, teacher_w, student_w, block_mask):
    block_size = student_w.shape[0] // block_mask.shape[0]
    expand = jnp.repeat(jnp.repeat(block_mask, block_size, axis=0), block_size, axis=1).astype(
        jnp.bfloat16
    )
    masked = student_w * expand
    half_full = lax.all_gather(acts, "tensor", axis=1, tiled=True)
    every_row = lax.all_gather(half_full, "sub", axis=0, tiled=True)
    teacher_cols = jnp.dot(every_row, teacher_w, preferred_element_type=jnp.float32).astype(
        jnp.bfloat16
    )
    teacher_own = lax.all_to_all(teacher_cols, "sub", split_axis=0, concat_axis=1, tiled=True)
    term_sums = jnp.dot(acts, masked, preferred_element_type=jnp.float32)
    student_own = lax.psum_scatter(term_sums, "tensor", scatter_dimension=1, tiled=True)
    teacher_f = teacher_own.astype(jnp.float32)
    difference = student_own - teacher_f
    numerator, denominator = lax.psum(
        (jnp.sum(difference * difference), jnp.sum(teacher_f * teacher_f)), ("tensor", "sub")
    )
    grad_out = (2.0 * 65536.0 / denominator * difference).astype(jnp.bfloat16)
    grad_full = lax.all_gather(grad_out, "tensor", axis=1, tiled=True)
    partial_value = lax.dot_general(
        acts, grad_full, (((0,), (0,)), ((), ())), preferred_element_type=jnp.float32
    )
    gradient = lax.psum(partial_value, "sub")
    return (gradient * expand.astype(jnp.float32), (numerator / denominator).reshape(1))


def solution(mesh):
    in_specs = (
        P(("copies", "sub"), "tensor"),
        P(None, ("tensor", "sub")),
        P("tensor", None),
        P("tensor", None),
    )
    out_specs = (P(("copies", "tensor"), None), P("copies"))
    return jax.shard_map(shards, mesh=mesh, in_specs=in_specs, out_specs=out_specs, check_vma=False)
```

profile of v0, /device:TPU:0, one launch (start us, length us, event | category | flops | bytes accessed | tf_op | source)
XLA Modules:
  0.0 450.1 jit_solution(2028806529028793379)
XLA Ops:
  7.2 0.0 all-gather.4.cloned.1.call-start
  7.2 0.7 all-gather.4.cloned.1.call-update
  7.9 0.0 all-gather.6.cloned.1.call-start
  7.9 54.2 %all-gather.4.cloned.1.call-done = bf16[128,8192]{1,0:T(8,128)(2,1)} async-done(((bf16[128,1024]{1,0:T(8,128)(2,1)}), bf16[128,8192]{1,0:T(8,128)(2,1)}) %all-gather.4.cloned.1.call-update) | async-done | bytes 2097168 | tf_op jit(solution)/shard_map/all_gather | solution.py:13
  62.2 0.0 all-gather.6.cloned.1.call-update
  62.2 0.0 reduce-scatter.2.cloned.1.call-start
  62.3 0.7 convert_element_type.35
  62.9 0.1 copy.6
  63.0 0.1 broadcast_in_dim.6
  63.2 22.6 %copy.7 = bf16[1024,8192]{0,1:T(8,128)(2,1)} copy(bf16[1024,8192]{1,0:T(8,128)(2,1)} %param.6) | data formatting | bytes 33554432 | tf_op args[2]
  85.8 9.8 %bitcast_multiply_fusion = bf16[1024,8192]{0,1:T(8,128)(2,1)S(1)} fusion(bf16[1024,8192]{0,1:T(8,128)(2,1)} %copy.7, bf16[1024,64]{0,1:T(8,128)(2,1)S(1)} %bitcast.29), kind=kLoop, calls=%fused_computation.1 | loop fusion | flops 8388608 | bytes 33685504 | tf_op jit(solution)/shard_map/mul | solution.py:12
  95.7 0.0 copy-done
  95.7 6.1 %convolution_bitcast_fusion.1 = f32[128,8192]{0,1:T(8,128)} fusion(bf16[1024,8192]{0,1:T(8,128)(2,1)S(1)} %bitcast_multiply_fusion, bf16[128,1024]{1,0:T(8,128)(2,1)S(1)} %copy-done), kind=kOutput, calls=%fused_computation.3 | convolution fusion | flops 2147483648 | bytes 21233664 | tf_op jit(solution)/shard_map/dot_general | solution.py:19
  101.8 0.0 reduce-scatter.2.cloned.1.call-update
  101.8 0.0 all-gather.8.cloned.1.call-start
  101.9 0.0 all-gather.6.cloned.1.call-done
  101.9 7.0 %convolution_convert_fusion = bf16[256,512]{1,0:T(8,128)(2,1)S(1)} fusion(bf16[256,8192]{1,0:T(8,128)(2,1)} %all-gather.6.cloned.1.call-done, bf16[8192,512]{1,0:T(8,128)(2,1)} %param.5), kind=kOutput, calls=%fused_computation.4 | convolution fusion | flops 2147614720 | bytes 12845056 | tf_op jit(solution)/shard_map/dot_general | solution.py:15
  108.9 3.9 all_to_all.13
  112.9 0.2 copy.8
  113.1 0.7 fusion
  113.9 74.8 %reduce-scatter.2.cloned.1.call-done = f32[128,1024]{0,1:T(8,128)} async-done(((f32[128,8192]{0,1:T(8,128)}), f32[128,1024]{0,1:T(8,128)}) %reduce-scatter.2.cloned.1.call-update) | async-done | bytes 524304 | tf_op jit(solution)/shard_map/reduce_scatter | solution.py:20
  188.6 1.8 multiply_reduce_fusion
  190.4 32.9 %all-reduce = (f32[]{:T(128)}, f32[]{:T(128)}) all-reduce(f32[]{:T(128)} %fusion, f32[]{:T(128)} %multiply_reduce_fusion), channel_id=1, replica_groups=mesh['copies'=2,'tensor'=8,'sub'=2] {'tensor','sub'}, use_global_device_ids=true, to_apply=%region_1.0 | all-reduce | flops 2 | bytes 16 | tf_op jit(solution)/shard_map/psum | solution.py:23
  224.0 1.8 multiply_convert_fusion
  225.8 0.0 all-gather.8.cloned.1.call-update
  225.8 0.0 all-reduce.3.cloned.1.call-start
  225.8 46.6 %all-gather.8.cloned.1.call-done = bf16[128,8192]{0,1:T(8,128)(2,1)} async-done(((bf16[128,1024]{0,1:T(8,128)(2,1)}), bf16[128,8192]{0,1:T(8,128)(2,1)}) %all-gather.8.cloned.1.call-update) | async-done | bytes 2097168 | tf_op jit(solution)/shard_map/all_gather | solution.py:27
  272.5 15.6 %convolution_bitcast_fusion = f32[1024,8192]{0,1:T(8,128)} fusion(bf16[128,8192]{0,1:T(8,128)(2,1)} %all-gather.8.cloned.1.call-done, bf16[128,1024]{1,0:T(8,128)(2,1)S(1)} %copy-done), kind=kOutput, calls=%fused_computation.2 | convolution fusion | flops 2147483648 | bytes 35913728 | tf_op jit(solution)/shard_map/dot_general | solution.py:28
  288.1 0.0 all-reduce.3.cloned.1.call-update
  289.4 99.5 %all-reduce.3.cloned.1.call-done = f32[1024,8192]{0,1:T(8,128)} async-done(((f32[1024,8192]{0,1:T(8,128)}), f32[1024,8192]{0,1:T(8,128)}) %all-reduce.3.cloned.1.call-update) | async-done | bytes 33554448 | tf_op jit(solution)/shard_map/psum | solution.py:31
  388.8 22.5 %convert_multiply_fusion = f32[1024,8192]{0,1:T(8,128)} fusion(f32[1024,8192]{0,1:T(8,128)} %all-reduce.3.cloned.1.call-done, bf16[1024,64]{0,1:T(8,128)(2,1)S(1)} %bitcast.30), kind=kLoop, calls=%fused_computation | loop fusion | flops 16777216 | bytes 67239936 | tf_op jit(solution)/shard_map/mul | solution.py:32
  411.4 31.1 %copy.9 = f32[1024,8192]{1,0:T(8,128)} copy(f32[1024,8192]{0,1:T(8,128)} %convert_multiply_fusion) | data formatting | bytes 67108864
  (3 shorter events, 0.1 us)
Async XLA Ops:
  7.2 55.0 %all-gather.4.cloned.1.call-start = ((), (), s32[]{:S(2)}) async-start(), calls=%async_computation.2 | async-start | bytes 2359296 | tf_op jit(solution)/shard_map/all_gather | solution.py:13
  7.9 94.0 %all-gather.6.cloned.1.call-start = ((), (), s32[]{:S(2)}) async-start(), calls=%async_computation.3 | async-start | bytes 6291456 | tf_op jit(solution)/shard_map/all_gather | solution.py:14
  62.2 126.4 %reduce-scatter.2.cloned.1.call-start = ((), (), s32[]{:S(2)}) async-start(), calls=%async_computation.4 | async-start | bytes 4718592 | tf_op jit(solution)/shard_map/reduce_scatter | solution.py:20
  85.8 9.8 %copy-start = (bf16[128,1024]{1,0:T(8,128)(2,1)S(1)}, bf16[128,1024]{1,0:T(8,128)(2,1)}, u32[]{:S(2)}) copy-start(bf16[128,1024]{1,0:T(8,128)(2,1)} %param.4) | copy-start | bytes 786436
  101.8 170.6 %all-gather.8.cloned.1.call-start = ((), (), s32[]{:S(2)}) async-start(), calls=%async_computation.5 | async-start | bytes 2359296 | tf_op jit(solution)/shard_map/all_gather | solution.py:27
  225.8 163.1 %all-reduce.3.cloned.1.call-start = ((), (), s32[]{:S(2)}) async-start(), calls=%async_computation.6 | async-start | bytes 67108864 | tf_op jit(solution)/shard_map/psum | solution.py:31
Sparse Core Ops, SparseCore 0:
  10.2 51.9 all-gather.3
  63.7 12.1 all-gather.5
  102.0 86.5 reduce-scatter.1
  225.9 46.5 all-gather.7
  288.2 100.5 all-reduce.2
where the time goes:
time: 452 us; the launch traced here: 450 us
  waiting for transfers between devices  276 us (61%)
  local copies, waits for them, and re-layouts  54.1 us (12%)
  other arithmetic  37.4 us (8%)
  blocking collectives  36.8 us (8%)
  matrix products  28.7 us (6%)
  between operations  17 us (4%)
    psum x1, waiting for transfers between devices, shards(): gradient = lax.psum(partial_value, 'sub')  99.5 us
    reduce_scatter x1, waiting for transfers between devices, shards(): lax.psum_scatter(term_sums, 'tensor', scatter_dimension=1, tiled=True)  74.8 us
    all_gather x1, waiting for transfers between devices, shards(): half_full = lax.all_gather(acts, 'tensor', axis=1, tiled=True)  54.2 us
    unnamed x5, local copies, waits for them, and re-layouts  53.7 us
    all_gather x1, waiting for transfers between devices, shards(): grad_full = lax.all_gather(grad_out, 'tensor', axis=1, tiled=True)  46.6 us
    psum x1, blocking collectives, shards(): lax.psum((jnp.sum(difference * difference), jnp.sum(teacher_f * teacher_f...  32.9 us
    mul x1, other arithmetic, shards(): gradient * expand.astype(jnp.float32)  22.5 us
    dot_general x1, matrix products, shards(): lax.dot_general(acts, grad_full, (((0,), (0,)), ((), ())), preferred_elem...  15.6 us
  transfers between devices with their start and end apart: 5, of which 4 were waited for; matrix products, arithmetic and copies ran while one was open for 11% of the time, Pallas kernels for 0%

commit v1 on v0

v1 whole, which is shorter than its diff:
```python
import functools

import jax
import jax.numpy as jnp
from jax import lax
from jax.experimental import pallas as pl
from jax.experimental.pallas import tpu as pltpu
from jax.sharding import PartitionSpec as P

MESH = pl.DeviceIdType.MESH
F32 = jnp.float32
BF16 = jnp.bfloat16


def tensor_of(pos, n):
    high = pos // (n // 2)
    return 2 * (pos + high * (n - 1 - 2 * pos)) + high


def exchange_kernel(
    n, blk, acts_ref, tw_ref, sw_ref, mask_ref, diff_out, acts_out, stat_out,
    abuf, swbuf, twbuf, pbuf, tacc, rs_out, rs_in, dbuf, sbuf,
    in_sem, sw_sem, tw_sem, ag_send, ag_recv, sib_send, sib_recv, rs_send, rs_recv,
    dg_send, dg_recv, dsib_send, dsib_recv, out_sem,
):
    t = lax.axis_index("tensor")
    s = lax.axis_index("sub")
    z = t // 2
    x = t % 2
    r = z + x * (n - 1 - 2 * z)
    right = {"tensor": tensor_of((r + 1) % n, n)}
    left = {"tensor": tensor_of((r + n - 1) % n, n)}
    other = {"sub": 1 - s}
    rows = acts_ref.shape[0]
    half = acts_ref.shape[1] // 2
    cols = tw_ref.shape[1]
    mine = pl.ds(pl.multiple_of(s * rows, rows), rows)
    theirs = pl.ds(pl.multiple_of((1 - s) * rows, rows), rows)
    ways = (right, left)

    def source(w, k):
        return tensor_of((r + n - k) % n if w == 0 else (r + k) % n, n)

    def student_pos(w, k):
        return (r + n - 1 - k) % n if w == 0 else (r + (1 + k) % (n // 2)) % n

    def own_copy(w):
        return pltpu.make_async_copy(
            acts_ref.at[:, pl.ds(w * half, half)], abuf.at[t, w, mine], in_sem.at[w]
        )

    def sw_copy(w, k):
        col = (2 * tensor_of(student_pos(w, k), n) + s) * cols
        return pltpu.make_async_copy(
            sw_ref.at[:, pl.ds(pl.multiple_of(col, cols), cols)], swbuf.at[w, k], sw_sem.at[w, k]
        )

    def tw_copy(w, k):
        row = (2 * source(w, k) + w) * half
        return pltpu.make_async_copy(
            tw_ref.at[pl.ds(pl.multiple_of(row, half), half)], twbuf.at[w, k], tw_sem.at[w, k]
        )

    def remote(src, dst, send, recv, where):
        return pltpu.make_async_remote_copy(
            src_ref=src, dst_ref=dst, send_sem=send, recv_sem=recv,
            device_id=where, device_id_type=MESH,
        )

    def ag_copy(w, k, at):
        piece = abuf.at[source(w, at), w, mine]
        return remote(piece, piece, ag_send.at[w, k], ag_recv.at[w, k], ways[w])

    def sib_copy(w, k, whose):
        piece = abuf.at[source(w, k), w, whose]
        return remote(piece, piece, sib_send.at[w, k], sib_recv.at[w, k], other)

    def rs_copy(w, k):
        return remote(
            rs_out.at[w, k], rs_in.at[w, k], rs_send.at[w, k], rs_recv.at[w, k], ways[w]
        )

    def dg_piece(w, k, core):
        block = 2 * source(w % 2, k) + core
        return sbuf.at[block] if w == 2 else dbuf.at[block, w]

    def dg_copy(w, k, at):
        piece = dg_piece(w, at, s)
        return remote(piece, piece, dg_send.at[w, k], dg_recv.at[w, k], ways[w % 2])

    def dsib_copy(w, k, core):
        piece = dg_piece(w, k, core)
        return remote(piece, piece, dsib_send.at[w, k], dsib_recv.at[w, k], other)

    for w in range(2):
        own_copy(w).start()

    def load_student(k, c):
        sw_copy(0, k).start()
        sw_copy(1, k).start()
        return c

    def load_teacher(k, c):
        tw_copy(0, k).start()
        tw_copy(1, k).start()
        return c

    lax.fori_loop(0, n // 2, load_student, 0)
    lax.fori_loop(0, n, load_teacher, 0)

    barrier = pltpu.get_barrier_semaphore()
    for where in (right, left, other):
        pl.semaphore_signal(barrier, inc=1, device_id=where, device_id_type=MESH)
    pl.semaphore_wait(barrier, 3)

    tacc[...] = jnp.zeros_like(tacc)
    for w in range(2):
        own_copy(w).wait()

    def student(w, k):
        sw_copy(w, k).wait()
        pos = student_pos(w, k)
        first = (2 * tensor_of(pos, n) + s) * (cols // blk)
        for i in range(2 * half // blk):
            for j in range(cols // blk):
                keep = jnp.full((blk, blk), mask_ref[i, first + j].astype(F32), F32).astype(BF16)
                at = (w, k, pl.ds(i * blk, blk), pl.ds(j * blk, blk))
                swbuf[at] = swbuf[at] * keep
        total = jnp.dot(abuf[t, 0], swbuf[w, k, :half], preferred_element_type=F32)
        total += jnp.dot(abuf[t, 1], swbuf[w, k, half:], preferred_element_type=F32)
        pbuf[pos] = total

    def step(k, c):
        @pl.when(k > 0)
        def _():
            for w in range(2):
                ag_copy(w, k - 1, k).wait_recv()

        @pl.when(k < n - 1)
        def _():
            for w in range(2):
                ag_copy(w, k, k).start()

        for w in range(2):
            sib_copy(w, k, mine).start()

        @pl.when(k == 0)
        def _():
            for w in range(2):
                sib_copy(w, 0, theirs).wait_recv()

        @pl.when(k < n // 2)
        def _():
            for w in range(2):
                student(w, k)

        @pl.when(k < n - 1)
        def _():
            for w in range(2):
                pos = (r + n - 1 - k) % n if w == 0 else (r + 1 + k) % n
                part = pbuf.at[pos, pl.ds(w * rows, rows)]

                @pl.when(k == 0)
                def _():
                    rs_out[w, k] = part[...].astype(BF16)

                @pl.when(k > 0)
                def _():
                    rs_copy(w, k - 1).wait_recv()
                    rs_out[w, k] = (part[...] + rs_in[w, k - 1].astype(F32)).astype(BF16)

                rs_copy(w, k).start()

        @pl.when(k > 0)
        def _():
            for w in range(2):
                sib_copy(w, k, theirs).wait_recv()

        for w in range(2):
            tw_copy(w, k).wait()
        total = jnp.dot(abuf[source(0, k), 0], twbuf[0, k], preferred_element_type=F32)
        total += jnp.dot(abuf[source(1, k), 1], twbuf[1, k], preferred_element_type=F32)
        tacc[...] += total
        return c

    lax.fori_loop(0, n, step, 0)

    squares = []
    for w in range(2):
        rs_copy(w, n - 2).wait_recv()
        part = slice(w * rows, (w + 1) * rows)
        teacher = tacc[part].astype(BF16).astype(F32)
        difference = pbuf[r, part] + rs_in[w, n - 2].astype(F32) - teacher
        dbuf[2 * t + s, w] = difference.astype(BF16)
        squares.append((jnp.sum(difference * difference), jnp.sum(teacher * teacher)))
    index = lax.broadcasted_iota(jnp.int32, sbuf.shape[1:], 0)
    sbuf[2 * t + s] = jnp.where(
        index == 0, squares[0][0] + squares[1][0], squares[0][1] + squares[1][1]
    )

    def spread(k, c):
        @pl.when(k > 0)
        def _():
            for w in range(3):
                dg_copy(w, k - 1, k).wait_recv()

        @pl.when(k < n - 1)
        def _():
            for w in range(3):
                dg_copy(w, k, k).start()

        for w in range(3):
            dsib_copy(w, k, s).start()
        return c

    lax.fori_loop(0, n, spread, 0)

    def arrived(k, c):
        for w in range(3):
            dsib_copy(w, k, 1 - s).wait_recv()
        return c

    lax.fori_loop(0, n, arrived, 0)
    results = [
        pltpu.make_async_copy(dbuf, diff_out, out_sem.at[0]),
        pltpu.make_async_copy(abuf.at[t], acts_out, out_sem.at[1]),
        pltpu.make_async_copy(sbuf, stat_out, out_sem.at[2]),
    ]
    for copy in results:
        copy.start()

    def drain(k, c):
        for w in range(2):
            sib_copy(w, k, mine).wait_send()

            @pl.when(k < n - 1)
            def _():
                ag_copy(w, k, k).wait_send()
                rs_copy(w, k).wait_send()

        for w in range(3):
            dsib_copy(w, k, s).wait_send()

            @pl.when(k < n - 1)
            def _():
                dg_copy(w, k, k).wait_send()

        return c

    lax.fori_loop(0, n, drain, 0)
    for copy in results:
        copy.wait()


def exchange(n, acts, teacher_w, student_w, block_mask):
    rows, width = acts.shape
    half = width // 2
    cols = teacher_w.shape[1]
    blk = width // block_mask.shape[0]
    dma = pltpu.SemaphoreType.DMA
    anywhere = pl.BlockSpec(memory_space=pl.ANY)
    return pl.pallas_call(
        functools.partial(exchange_kernel, n, blk),
        out_shape=(
            jax.ShapeDtypeStruct((2 * n, 2, rows, cols), BF16),
            jax.ShapeDtypeStruct((2, 2 * rows, half), BF16),
            jax.ShapeDtypeStruct((2 * n, 8, 128), F32),
        ),
        in_specs=[anywhere] * 3 + [pl.BlockSpec(memory_space=pltpu.SMEM)],
        out_specs=(anywhere,) * 3,
        scratch_shapes=[
            pltpu.VMEM((n, 2, 2 * rows, half), BF16),
            pltpu.VMEM((2, n // 2, width, cols), BF16),
            pltpu.VMEM((2, n, half, cols), BF16),
            pltpu.VMEM((n, 2 * rows, cols), F32),
            pltpu.VMEM((2 * rows, cols), F32),
            pltpu.VMEM((2, n - 1, rows, cols), BF16),
            pltpu.VMEM((2, n - 1, rows, cols), BF16),
            pltpu.VMEM((2 * n, 2, rows, cols), BF16),
            pltpu.VMEM((2 * n, 8, 128), F32),
            dma((2,)), dma((2, n // 2)), dma((2, n)),
            dma((2, n - 1)), dma((2, n - 1)), dma((2, n)), dma((2, n)),
            dma((2, n - 1)), dma((2, n - 1)),
            dma((3, n - 1)), dma((3, n - 1)), dma((3, n)), dma((3, n)),
            dma((3,)),
        ],
        compiler_params=pltpu.CompilerParams(
            collective_id=0, has_side_effects=True, vmem_limit_bytes=50 * 2**20
        ),
        cost_estimate=pl.CostEstimate(
            flops=8 * rows * width * cols * n, bytes_accessed=4 * width * cols * n,
            transcendentals=0,
        ),
    )(acts, teacher_w, student_w, block_mask)


def gradient_kernel(blk, acts_ref, diff_ref, stat_ref, mask_ref, grad_ref, loss_ref, turned, scale):
    half = acts_ref.shape[2]
    cols = diff_ref.shape[2]
    at = pl.program_id(0)

    @pl.when(at == 0)
    def _():
        for w in range(2):
            turned[w] = acts_ref[w].astype(F32).T.astype(BF16)
        numerator = jnp.sum(stat_ref[:, 0, :]) / 128.0
        denominator = jnp.sum(stat_ref[:, 1, :]) / 128.0
        scale[0] = 2.0 * 65536.0 / denominator
        loss_ref[0] = numerator / denominator

    for w in range(2):
        value = jnp.dot(turned[w], diff_ref[0], preferred_element_type=F32)
        for i in range(half // blk):
            for j in range(cols // blk):
                row = w * (half // blk) + i
                kept = mask_ref[row, at * (cols // blk) + j].astype(F32) * scale[0]
                grad_ref[pl.ds(row * blk, blk), pl.ds(j * blk, blk)] = (
                    value[i * blk : (i + 1) * blk, j * blk : (j + 1) * blk] * kept
                )


def gradient(acts, diff, stats, block_mask):
    _, tokens, half = acts.shape
    blocks, _, cols = diff.shape
    blk = 2 * half // block_mask.shape[0]
    return pl.pallas_call(
        functools.partial(gradient_kernel, blk),
        grid=(blocks,),
        out_shape=(
            jax.ShapeDtypeStruct((2 * half, blocks * cols), F32),
            jax.ShapeDtypeStruct((1,), F32),
        ),
        in_specs=[
            pl.BlockSpec((2, tokens, half), lambda b: (0, 0, 0)),
            pl.BlockSpec((1, tokens, cols), lambda b: (b, 0, 0)),
            pl.BlockSpec(stats.shape, lambda b: (0, 0, 0)),
            pl.BlockSpec(memory_space=pltpu.SMEM),
        ],
        out_specs=(
            pl.BlockSpec((2 * half, cols), lambda b: (0, b)),
            pl.BlockSpec(memory_space=pltpu.SMEM),
        ),
        scratch_shapes=[pltpu.VMEM((2, half, tokens), BF16), pltpu.SMEM((1,), F32)],
        compiler_params=pltpu.CompilerParams(vmem_limit_bytes=40 * 2**20),
    )(acts, diff, stats, block_mask)


def ring_shards(n, acts, teacher_w, student_w, block_mask):
    diff, both, stats = exchange(n, acts, teacher_w, student_w, block_mask)
    diff = diff.reshape(diff.shape[0], -1, diff.shape[-1])
    return gradient(both, diff, stats, block_mask)


def shards(n, acts, teacher_w, student_w, block_mask):
    blk = student_w.shape[0] // block_mask.shape[0]
    expand = jnp.repeat(jnp.repeat(block_mask, blk, axis=0), blk, axis=1).astype(BF16)
    masked = student_w * expand
    s = lax.axis_index("sub")
    cols = teacher_w.shape[1]
    both = lax.all_gather(acts, "sub", axis=0, tiled=True)
    full = lax.all_gather(both, "tensor", axis=1, tiled=True)
    teacher = jnp.dot(full, teacher_w, preferred_element_type=F32).astype(BF16).astype(F32)
    own = lax.dynamic_index_in_dim(masked.reshape(-1, n, 2, cols), s, 2, keepdims=False)
    terms = jnp.dot(both, own.reshape(-1, n * cols), preferred_element_type=F32)
    student = lax.psum_scatter(terms, "tensor", scatter_dimension=1, tiled=True)
    difference = student - teacher
    numerator, denominator = lax.psum(
        (jnp.sum(difference * difference), jnp.sum(teacher * teacher)), ("tensor", "sub")
    )
    grad_out = (2.0 * 65536.0 / denominator * difference).astype(BF16)
    grad_full = lax.all_gather(grad_out, ("tensor", "sub"), axis=1, tiled=True)
    value = lax.dot_general(both, grad_full, (((0,), (0,)), ((), ())), preferred_element_type=F32)
    return value * expand.astype(F32), (numerator / denominator).reshape(1)


def solution(mesh):
    n, cores = mesh.shape["tensor"], mesh.shape["sub"]

    def run(acts, teacher_w, student_w, block_mask):
        cols = teacher_w.shape[1] // (n * cores)
        half = acts.shape[1] // n // 2
        ring = cores == 2 and 4 <= n <= 16 and n % 4 == 0 and cols % 128 == 0 and half % 128 == 0
        return jax.shard_map(
            functools.partial(ring_shards if ring else shards, n),
            mesh=mesh,
            in_specs=(
                P(("copies", "sub"), "tensor"),
                P(None, ("tensor", "sub")),
                P("tensor", None),
                P("tensor", None),
            ),
            out_specs=(P(("copies", "tensor"), None), P("copies")),
            check_vma=False,
        )(acts, teacher_w, student_w, block_mask)

    return run
```

time: 452 us -> 104 us (0.23)
  waiting for transfers between devices: 276 us -> 0 us
  Pallas kernels: 0 us -> 98.1 us
  local copies, waits for them, and re-layouts: 54.1 us -> 3.81 us
  other arithmetic: 37.4 us -> 0 us
  blocking collectives: 36.8 us -> 0 us
  matrix products: 28.7 us -> 0 us
  between operations: 17 us -> 0.66 us
    all_gather x3 -> x0, waiting for transfers between devices: 101 us -> none  [the longest x1 54.2 us: shards(): half_full = lax.all_gather(acts, 'tensor', axis=1, tiled=True)]
    psum x1 -> x0, waiting for transfers between devices: 99.5 us -> none  [shards(): gradient = lax.psum(partial_value, 'sub')]
    pallas_call x0 -> x2, Pallas kernels: none -> 98.1 us  [the longest x1 82.4 us: exchange(): pl.pallas_call(functools.partial(exchange_kernel, n, blk), out_shape=(jax...]
    reduce_scatter x1 -> x0, waiting for transfers between devices: 74.8 us -> none  [shards(): lax.psum_scatter(term_sums, 'tensor', scatter_dimension=1, tiled=True)]
    unnamed x5 -> x6, local copies, waits for them, and re-layouts: 53.7 us -> 3.81 us
    psum x1 -> x0, blocking collectives: 32.9 us -> none  [shards(): lax.psum((jnp.sum(difference * difference), jnp.sum(teacher_f * teacher_f...]
    mul x2 -> x0, other arithmetic: 32.4 us -> none  [the longest x1 22.5 us: shards(): gradient * expand.astype(jnp.float32)]
    dot_general x3 -> x0, matrix products: 28.7 us -> none  [the longest x1 15.6 us: shards(): lax.dot_general(acts, grad_full, (((0,), (0,)), ((), ())), preferred_elem...]
  transfers between devices with their start and end apart: 5 -> 0, of which waited for: 4 -> 0; matrix products, arithmetic and copies ran while one was open for 11% -> 0% of each run, Pallas kernels for 0% -> 0%
where the time goes in v1:
time: 104 us; the launch traced here: 103 us
  Pallas kernels  98.1 us (94%)
  local copies, waits for them, and re-layouts  3.81 us (4%)
    pallas_call x1, Pallas kernels, exchange(): pl.pallas_call(functools.partial(exchange_kernel, n, blk), out_shape=(jax...  82.4 us
    pallas_call x1, Pallas kernels, gradient(): pl.pallas_call(functools.partial(gradient_kernel, blk), grid=(blocks,), o...  15.7 us
    unnamed x6, local copies, waits for them, and re-layouts  3.81 us

profile of v1, /device:TPU:0, one launch (start us, length us, event | category | flops | bytes accessed | tf_op | source)
XLA Modules:
  0.0 102.5 jit_solution(16538444148194791846)
XLA Ops:
  0.6 0.0 copy-start.1
  0.6 0.9 copy-done.1
  1.6 0.0 copy-start.2
  1.6 0.7 copy-done.2
  2.3 82.4 %shard_map.59 = (bf16[16,2,128,512]{3,2,1,0:T(8,128)(2,1)}, bf16[2,256,512]{2,1,0:T(8,128)(2,1)S(1)}, f32[16,8,128]{2,1,0:T(8,128)S(1)}) custom-call(bf16[128,1024]{1,0:T(8,128)(2,1)S(1)} %copy-done.1, bf16[8192,512]{1,0:T(8,128)(2,1)} %tw_ref.1, bf16[1024,8192]{1,0:T(8,128)(2,1)} %sw_ref.1, s32[8,64]{1,0:T(8,128)S(1)} %copy-done.2), custom_call_target="tpu_custom_call" | custom-call | flops 4294967296 | bytes 16777216 | tf_op jit(solution)/shard_map/pallas_call | solution.py:262
  84.7 0.0 copy-start
  84.7 2.2 %copy-done = bf16[16,2,128,512]{3,2,1,0:T(8,128)(2,1)S(1)} copy-done((bf16[16,2,128,512]{3,2,1,0:T(8,128)(2,1)S(1)}, bf16[16,2,128,512]{3,2,1,0:T(8,128)(2,1)}, u32[]{:S(2)}) %copy-start) | copy-done | bytes 4194328
  86.9 15.7 %shard_map.60 = (f32[1024,8192]{1,0:T(8,128)}, f32[1]{0:T(128)}) custom-call(bf16[2,256,512]{2,1,0:T(8,128)(2,1)S(1)} %get-tuple-element.5.acts_ref, bf16[16,256,512]{2,1,0:T(8,128)(2,1)S(1)} %bitcast.1, f32[16,8,128]{2,1,0:T(8,128)S(1)} %get-tuple-element.7.stat_ref, s32[8,64]{1,0:T(8,128)S(1)} %copy-done.2), custom_call_target="tpu_custom_call" | custom-call | tf_op jit(solution)/shard_map/pallas_call | solution.py:326
Async XLA Ops:
  0.6 1.0 copy-start.1
  1.6 0.7 copy-start.2
  84.7 2.2 %copy-start = (bf16[16,2,128,512]{3,2,1,0:T(8,128)(2,1)S(1)}, bf16[16,2,128,512]{3,2,1,0:T(8,128)(2,1)}, u32[]{:S(2)}) copy-start(bf16[16,2,128,512]{3,2,1,0:T(8,128)(2,1)} %get-tuple-element.6) | copy-start | bytes 12582916
